TPU v7x, 128 devices: a whole 4x4x4 slice. The times are simulated.
128 devices in a mesh: section: 4 (over y), kv: 32 (over x, z, core).
Axes of the slice: x: 4, y: 4, z: 4, core: 2. Of those that a mesh axis runs over, the one named last changes fastest.
Arguments:
- hidden: bfloat16 [4, 64, 8192], P('section'), may hold values from -6 to 6
- norm_gain: float32 [4, 8192], P('section'), may hold values from 0.1 to 1.9
- query_weight: bfloat16 [4, 8192, 8192], P('section', None, 'kv'), may hold values from -0.0625 to 0.0625
- key_cache: bfloat16 [4, 384, 256, 1024], P('section', 'kv')
- value_cache: bfloat16 [4, 384, 256, 1024], P('section', 'kv'), may hold values from -6 to 6
- out_weight: bfloat16 [4, 8192, 8192], P('section', 'kv'), may hold values from -0.0625 to 0.0625
- block_pos: int32 [384], P('kv'), may hold values from 0 to 383, each once
- lengths: int32 [32], replicated, may hold values from 1 to 98304, as said below
- span_start: int32 [1], replicated, may hold values from 0 to 98272
Outputs:
- next_hidden: bfloat16 [4, 64, 8192], P('section', 'kv')
Inputs may be any that keep to these rules, and one draw needn't show every extreme that they name: `block_pos`: every context block index appears in exactly one slot. `lengths`: some decode row reads the whole context.
All inputs are finite; a program needn't handle non-finite values.
Results may differ from a plain program's by a relative error of at most 0.015.
Values may be sent and summed in bfloat16 or wider, within the bound.
A program may use at most 320 MiB of HBM per device.

v0:
```python
import jax
import jax.numpy as jnp
from jax import lax
from jax.sharding import PartitionSpec as P

HQ = 64
KVH = 8
HD = 128


def merged(value, axis, join):
    pieces = jax.tree.map(lambda part: lax.all_gather(part, axis), value)
    head = jax.tree.map(lambda part: part[0], pieces)
    tail = jax.tree.map(lambda part: part[1:], pieces)
    total, _ = lax.scan(lambda total, piece: (join(total, piece), None), head, tail)
    return total


def shifted(array, axis, by):
    peers = lax.axis_size(axis)
    return lax.ppermute(array, axis, [(i, (i + by) % peers) for i in range(peers)])


def join_partials(earlier, later):
    sums_a, peak_a, total_a = earlier
    sums_b, peak_b, total_b = later
    peak = jnp.maximum(peak_a, peak_b)
    weight_a = jnp.exp(peak_a - peak)
    weight_b = jnp.exp(peak_b - peak)
    return (
        sums_a * weight_a[..., None] + sums_b * weight_b[..., None],
        peak,
        total_a * weight_a + total_b * weight_b,
    )


def local(
    hidden,
    norm_gain,
    query_weight,
    key_cache,
    value_cache,
    out_weight,
    block_pos,
    lengths,
    span_start,
):
    row_count = hidden.shape[1]
    group = HQ // KVH
    kv_count = lax.axis_size("kv")
    my_index = lax.axis_index("kv")
    heads_here = HQ // kv_count
    share = row_count // kv_count
    states = hidden[0].astype(jnp.float32)
    scale = lax.rsqrt(jnp.mean(states * states, axis=1, keepdims=True) + 1e-05)
    normed = (states * scale * norm_gain[0][None, :]).astype(jnp.bfloat16)
    local_q = jnp.dot(normed, query_weight[0], preferred_element_type=jnp.float32).astype(
        jnp.bfloat16
    )
    queries = lax.all_gather(local_q, "kv", axis=1, tiled=True)
    slot_count = key_cache.shape[1] * key_cache.shape[2]
    positions = (
        block_pos[:, None] * key_cache.shape[2]
        + jnp.arange(key_cache.shape[2], dtype=jnp.int32)[None, :]
    ).reshape(-1)
    limits = jnp.concatenate(
        [span_start[0] + jnp.arange(row_count - lengths.shape[0], dtype=jnp.int32) + 1, lengths]
    )
    allowed = positions[None, :] < limits[:, None]
    query_heads = jnp.moveaxis(queries.reshape(row_count, KVH, group, HD), 1, 0)
    key_heads = jnp.moveaxis(key_cache[0].reshape(slot_count, KVH, HD), 1, 0)
    value_heads = jnp.moveaxis(value_cache[0].reshape(slot_count, KVH, HD), 1, 0)

    def per_head(operands):
        query_group, key_head, value_head = operands
        scores = jnp.einsum(
            "rgd,cd->rgc", query_group, key_head, preferred_element_type=jnp.float32
        ) * HD ** (-0.5)
        masked = jnp.where(allowed[:, None, :], scores, jnp.float32(-1e30))
        peak = jnp.max(masked, axis=2)
        weights = jnp.where(
            allowed[:, None, :], jnp.exp(scores - peak[..., None]), jnp.float32(0.0)
        )
        total = jnp.sum(weights, axis=2)
        summed = jnp.einsum(
            "rgc,cd->rgd",
            weights.astype(jnp.bfloat16),
            value_head,
            preferred_element_type=jnp.float32,
        )
        return (summed, peak, total)

    summed, peak, total = lax.map(per_head, (query_heads, key_heads, value_heads))
    summed = jnp.moveaxis(summed, 0, 1).reshape(row_count, HQ, HD)
    peak = jnp.moveaxis(peak, 0, 1).reshape(row_count, HQ)
    total = jnp.moveaxis(total, 0, 1).reshape(row_count, HQ)
    summed_all, peak_all, total_all = merged((summed, peak, total), "kv", join_partials)
    mine_sums = lax.dynamic_slice_in_dim(summed_all, my_index * heads_here, heads_here, 1)
    mine_total = lax.dynamic_slice_in_dim(total_all, my_index * heads_here, heads_here, 1)
    attended = mine_sums / mine_total[..., None]
    attended = attended.reshape(row_count, heads_here * HD).astype(jnp.bfloat16)
    term = jnp.dot(attended, out_weight[0], preferred_element_type=jnp.float32)
    whole_sum = lax.psum(term.astype(jnp.bfloat16), "kv").astype(jnp.float32)
    projected = lax.dynamic_slice_in_dim(whole_sum, my_index * share, share, 0)
    my_states = lax.dynamic_slice_in_dim(states, my_index * share, share, 0)
    updated = (my_states + projected).astype(jnp.bfloat16)[None]
    return shifted(updated, "section", 1)


def solution(mesh):
    placed = (
        P("section", None, None),
        P("section", None),
        P("section", None, "kv"),
        P("section", "kv", None, None),
        P("section", "kv", None, None),
        P("section", "kv", None),
        P("kv"),
        P(),
        P(),
    )
    return jax.shard_map(
        local, mesh=mesh, in_specs=placed, out_specs=P("section", "kv", None), check_vma=False
    )
```

profile of v0, /device:TPU:1, one launch (start us, length us, event | category | flops | bytes accessed | tf_op | source)
XLA Modules:
  0.0 633.6 jit_solution(14850751616569482481)
XLA Ops:
  8.1 4.0 fusion.30
  12.2 4.4 copy.45
  16.7 4.1 copy.30
  23.2 3.7 copy.31
  27.7 31.3 %all-gather.3.cloned.1.call-done = bf16[64,8192]{1,0:T(8,128)(2,1)} async-done(((bf16[64,256]{1,0:T(8,128)(2,1)}), bf16[64,8192]{1,0:T(8,128)(2,1)}) %all-gather.3.cloned.1.call-update) | async-done | bytes 1048592 | tf_op jit(solution)/shard_map/all_gather | solution.py:60
  60.7 94.5 %while.30 = (s32[]{:T(128)}, f32[8,64,8,128]{3,2,0,1:T(8,128)S(1)}, f32[8,64,8]{1,2,0:T(8,128)S(1)}, f32[8,64,8]{1,2,0:T(8,128)S(1)}, bf16[8,64,8,128]{3,2,1,0:T...) while((s32[]{:T(128)}, f32[8,64,8,128]{3,2,0,1:T(8,128)S(1)}, ...), condition=%wide.region_4.5_spmd.clone, body=%wide.region_1.4_spmd.clone.sunk | while | flops 822803456 | bytes 46870916 | solution.py:93
  60.9 2.9 select_reduce_fusion.2
  68.6 4.0 fusion.54
  80.4 4.0 fusion.54
  92.2 4.0 fusion.54
  104.0 4.0 fusion.54
  115.8 4.0 fusion.54
  120.0 2.9 select_reduce_fusion.2
  127.6 4.0 fusion.54
  139.4 4.0 fusion.54
  143.6 2.9 select_reduce_fusion.2
  151.2 4.0 fusion.54
  156.7 25.7 %all_gather.14 = f32[32,64,64]{2,1,0:T(8,128)S(1)} all-gather(f32[1,64,64]{2,1,0:T(8,128)S(1)} %copy.34), channel_id=1, replica_groups=mesh['section'=4,'kv'=32] {'kv'}, dimensions={0}, use_global_device_ids=true | all-gather | bytes 540672 | tf_op jit(solution)/shard_map/all_gather | solution.py:12
  182.5 23.8 %all_gather.15 = f32[32,64,64]{2,1,0:T(8,128)S(1)} all-gather(f32[1,64,64]{2,1,0:T(8,128)S(1)} %copy.36), channel_id=1, replica_groups=mesh['section'=4,'kv'=32] {'kv'}, dimensions={0}, use_global_device_ids=true | all-gather | bytes 540672 | tf_op jit(solution)/shard_map/all_gather | solution.py:12
  207.4 153.5 %all-gather.5.cloned.1.call-done = f32[32,64,64,128]{3,2,1,0:T(8,128)} async-done(((f32[1,64,64,128]{3,2,1,0:T(8,128)}), f32[32,64,64,128]{3,2,1,0:T(8,128)}) %all-gather.5.cloned.1.call-update) | async-done | bytes 67108880 | tf_op jit(solution)/shard_map/all_gather | solution.py:12
  360.9 42.6 %slice.28 = f32[31,64,64,128]{3,2,1,0:T(8,128)} slice(f32[32,64,64,128]{3,2,1,0:T(8,128)} %all-gather.5.cloned.1.call-done), slice={[1:32], [0:64], [0:64], [0:128]} | slice | bytes 130023424 | tf_op jit(solution)/shard_map/slice | solution.py:14
  405.2 108.4 %while.29 = (s32[]{:T(128)}, f32[64,64,128]{2,1,0:T(8,128)S(1)}, f32[64,64]{1,0:T(8,128)S(1)}, f32[64,64]{1,0:T(8,128)S(1)}, f32[31,64,64]{2,1,0:T(8,128)S(1)}, ...) while((s32[]{:T(128)}, f32[64,64,128]{2,1,0:T(8,128)S(1)}, f32[64,64]{1,0:T(8,128)S(1)}, ...), condition=%wide.region_6.7_spmd, body=%wide.region_5.6_spmd.sunk | while | flops 1597442 | bytes 6455389 | solution.py:15
  513.8 4.1 convolution_convert_fusion
  518.1 103.3 %all-reduce.2.cloned.1.call-done = bf16[64,8192]{1,0:T(8,128)(2,1)} async-done(((bf16[64,8192]{1,0:T(8,128)(2,1)}), bf16[64,8192]{1,0:T(8,128)(2,1)}) %all-reduce.2.cloned.1.call-update) | async-done | bytes 1048592 | tf_op jit(solution)/shard_map/psum | solution.py:103
  (169 shorter events, 177.7 us)
Async XLA Ops:
  6.5 52.5 %all-gather.3.cloned.1.call-start = ((), (), s32[]{:S(2)}) async-start(), calls=%async_computation | async-start | bytes 1081344 | tf_op jit(solution)/shard_map/all_gather | solution.py:60
  12.1 348.7 %all-gather.5.cloned.1.call-start = ((), (), s32[]{:S(2)}) async-start(), calls=%async_computation.1 | async-start | bytes 69206016 | tf_op jit(solution)/shard_map/all_gather | solution.py:12
  16.6 4.1 slice-start
  16.7 4.9 slice-start.1
  23.2 3.7 copy-start.3
  23.2 4.4 copy-start.4
  63.8 2.6 copy-start
  75.6 2.6 copy-start
  87.4 2.6 copy-start
  99.3 2.6 copy-start
  111.1 2.6 copy-start
  122.9 2.6 copy-start
  134.7 2.6 copy-start
  146.5 2.6 copy-start
  155.2 1.3 copy-start.2
  156.6 464.9 %all-reduce.2.cloned.1.call-start = ((), (), s32[]{:S(2)}) async-start(), calls=%async_computation.2 | async-start | bytes 2097152 | tf_op jit(solution)/shard_map/psum | solution.py:103
  513.6 4.4 copy-start.1
  622.4 4.0 collective-permute-start
Sparse Core Ops, SparseCore 0:
  12.3 46.7 all-gather.2
  156.7 204.1 all-gather.4
  518.1 103.2 all-reduce.1
where the time goes:
time: 638 us; the launch traced here: 634 us
  waiting for transfers between devices  291 us (46%)
  other arithmetic  128 us (20%)
  local copies, waits for them, and re-layouts  85.6 us (13%)
  matrix products  63.1 us (10%)
  blocking collectives  49.5 us (8%)
  between operations  14 us (2%)
    all_gather x1, waiting for transfers between devices, merged(): pieces = jax.tree.map(lambda part: lax.all_gather(part, axis), value)  153 us
    psum x1, waiting for transfers between devices, local(): whole_sum = lax.psum(term.astype(jnp.bfloat16), 'kv').astype(jnp.float32)  103 us
    add x31, other arithmetic, join_partials(): sums_a * weight_a[..., None] + sums_b * weight_b[..., None]  82.8 us
    all_gather x2, blocking collectives, merged(): pieces = jax.tree.map(lambda part: lax.all_gather(part, axis), value)  49.5 us
    slice x3, local copies, waits for them, and re-layouts, merged(): tail = jax.tree.map(lambda part: part[1:], pieces)  43.7 us
    dot_general x8, matrix products, per_head(): jnp.einsum('rgc,cd->rgd', weights.astype(jnp.bfloat16), value_head, prefe...  31.7 us
    all_gather x1, waiting for transfers between devices, local(): queries = lax.all_gather(local_q, 'kv', axis=1, tiled=True)  31.3 us
    add x31, other arithmetic, join_partials(): total_a * weight_a + total_b * weight_b  24.9 us
  transfers between devices with their start and end apart: 4, of which 4 were waited for; matrix products, arithmetic and copies ran while one was open for 2% of the time, Pallas kernels for 0%

commit v1 on v0

v1 whole, which is shorter than its diff:
```python
import functools
import math

import jax
import jax.numpy as jnp
from jax import lax
from jax.experimental import pallas as pl
from jax.experimental.pallas import tpu as pltpu
from jax.sharding import PartitionSpec as P

HD = 128
LOG2_SCALE = math.log2(math.e) / math.sqrt(HD)
HIDDEN_BY_MASK = -1e30
PEAK_FLOOR = -1e28
MESH = pl.DeviceIdType.MESH
BF16, F32, I32 = jnp.bfloat16, jnp.float32, jnp.int32


def dot(a, b, contract=((1,), (0,))):
    return lax.dot_general(a, b, (contract, ((), ())), preferred_element_type=F32)


def arrived(ref, sem):
    pltpu.make_async_copy(ref, ref, sem).wait()


def kernel(
    sections,
    kv_count,
    hid_h,
    gain_h,
    wq_h,
    key_h,
    value_h,
    wo_h,
    block_pos,
    lengths,
    span_start,
    out,
    hid,
    gain,
    wq,
    keys,
    values,
    wo,
    queries,
    onehot,
    bias,
    blocks,
    q_out,
    o_out,
    stat_out,
    o_in,
    stat_in,
    attended,
    acc,
    rs_out,
    rs_in,
    fin_out,
    fin_in,
    in_sem,
    wq_sem,
    own_sem,
    kv_send,
    kv_recv,
    block_sem,
    q_send,
    q_recv,
    o_send,
    o_recv,
    stat_send,
    stat_recv,
    att_sem,
    rs_send,
    rs_recv,
    fin_send,
    fin_recv,
):
    rows, width = hid.shape
    x_count = kv_count // 8
    chips = kv_count // 2
    slots, block = key_h.shape[1], key_h.shape[2]
    half = width // 2
    lanes = rs_out.shape[2]
    span = slots * block
    section = lax.axis_index("section")
    me = lax.axis_index("kv")
    chip = lax.div(me, 2)
    core = lax.rem(me, 2)
    other = 1 - core
    sibling = chip * 2 + other
    x = lax.div(chip, 4)
    z = lax.rem(chip, 4)
    side = lax.div(z, 2)
    place = lax.rem(z, 2) * 2 + core

    load_hid = pltpu.make_async_copy(hid_h.at[0], hid, in_sem.at[0])
    load_gain = pltpu.make_async_copy(gain_h, gain, in_sem.at[1])
    load_hid.start()
    load_gain.start()
    pieces = wq_sem.shape[0]
    deep = wq.shape[0] // pieces

    def load_wq(n):
        part = pl.ds(n * deep, deep)
        return pltpu.make_async_copy(wq_h.at[0, part], wq.at[part], wq_sem.at[n])

    for n in range(pieces):
        load_wq(n).start()

    barrier = pltpu.get_barrier_semaphore()

    def greet(n, carry):
        @pl.when(n != me)
        def _():
            pl.semaphore_signal(barrier, inc=1, device_id={"kv": n}, device_id_type=MESH)

        return carry

    lax.fori_loop(0, kv_count, greet, 0)
    after = lax.rem(section + 1, sections)
    before = lax.rem(section + sections - 1, sections)
    for there in (after, before):
        for c in range(2):
            pl.semaphore_signal(
                barrier,
                inc=1,
                device_id={"section": there, "kv": chip * 2 + c},
                device_id_type=MESH,
            )

    blocks[0] = jnp.zeros((16, 128), F32)
    for j in range(slots):
        blocks[0, j : j + 1, :] = jnp.full((1, 128), block_pos[j], I32).astype(F32)
    lane = lax.broadcasted_iota(I32, (1, 128), 1)
    prefill = rows - lengths.shape[0]
    limits = span_start[0] + lane + 1
    for r in range(lengths.shape[0]):
        limits = jnp.where(lane == prefill + r, lengths[r], limits)
    limits = limits.astype(F32)
    token = lax.broadcasted_iota(I32, (block, 128), 0).astype(F32)

    def mask_columns(which):
        for j in range(slots):
            position = blocks[which, j : j + 1, :] * float(block) + token
            bias[pl.ds((which * slots + j) * block, block), :] = jnp.where(
                position < limits, 0.0, HIDDEN_BY_MASK
            ).astype(BF16)

    mask_columns(0)
    wide = onehot.shape[0]
    onehot[...] = jnp.where(
        lax.rem(lax.broadcasted_iota(I32, (wide, 128), 0), rows)
        == lax.broadcasted_iota(I32, (wide, 128), 1),
        1.0,
        0.0,
    ).astype(BF16)

    pl.semaphore_wait(barrier, kv_count - 1 + 4)

    def to_sibling(src, dst, n):
        return pltpu.make_async_remote_copy(
            src_ref=src,
            dst_ref=dst,
            send_sem=kv_send.at[n],
            recv_sem=kv_recv.at[n],
            device_id={"kv": sibling},
            device_id_type=MESH,
        )

    def head_at(i):
        return lax.rem(x + i, x_count)

    def head_lanes(slot, c):
        return pl.ds(pl.multiple_of((slot * 2 + c) * HD, HD), HD)

    def swap_copies():
        copies = []
        for i in range(x_count):
            slot = head_at(i)
            for k, (src, dst) in enumerate(((key_h, keys), (value_h, values))):
                copies.append(
                    to_sibling(
                        src.at[0, :, :, head_lanes(slot, other)],
                        dst.at[slot, pl.ds(slots, slots)],
                        i * 2 + k,
                    )
                )
        copies.append(
            to_sibling(
                wo_h.at[0, :, pl.ds(pl.multiple_of(other * half, half), half)],
                wo.at[core],
                2 * x_count,
            )
        )
        return copies

    send_blocks = pltpu.make_async_remote_copy(
        src_ref=blocks.at[0],
        dst_ref=blocks.at[1],
        send_sem=block_sem.at[0],
        recv_sem=block_sem.at[1],
        device_id={"kv": sibling},
        device_id_type=MESH,
    )
    send_blocks.start()
    for copy in swap_copies():
        copy.start()

    def own_copies():
        copies = []
        for i in range(x_count):
            slot = head_at(i)
            for k, (src, dst) in enumerate(((key_h, keys), (value_h, values))):
                copies.append(
                    pltpu.make_async_copy(
                        src.at[0, :, :, head_lanes(slot, core)],
                        dst.at[slot, pl.ds(0, slots)],
                        own_sem.at[i * 2 + k],
                    )
                )
        copies.append(
            pltpu.make_async_copy(
                wo_h.at[0, :, pl.ds(pl.multiple_of(core * half, half), half)],
                wo.at[core],
                own_sem.at[2 * x_count],
            )
        )
        return copies

    load_hid.wait()
    load_gain.wait()
    step = min(1024, deep)
    squares = jnp.zeros((rows, 1), F32)
    for n in range(width // step):
        part = hid[:, n * step : (n + 1) * step].astype(F32)
        squares = squares + jnp.sum(part * part, axis=1, keepdims=True)
    scale = lax.rsqrt(squares / width + 1e-05)
    projected = jnp.zeros((rows, 2 * HD), F32)
    for n in range(width // step):
        if n * step % deep == 0:
            load_wq(n * step // deep).wait()
        part = pl.ds(n * step, step)
        normed = (hid[:, part].astype(F32) * scale * gain[:, part]).astype(BF16)
        projected = projected + dot(normed, wq[part, :])
    q_out[pl.ds(0, rows), :] = projected[:, :HD].astype(BF16)
    q_out[pl.ds(rows, rows), :] = projected[:, HD:].astype(BF16)

    pair = 2 * rows

    def q_target(n):
        to_x = lax.rem(x + x_count - lax.div(n, 4), x_count)
        to_z = lax.rem(z + n, 4)
        return to_x * 8 + to_z * 2 + side

    def q_place():
        return queries.at[x, pl.ds(pl.multiple_of(place * pair, pair), pair)]

    def q_copy(n):
        return pltpu.make_async_remote_copy(
            src_ref=q_out,
            dst_ref=q_place(),
            send_sem=q_send.at[n],
            recv_sem=q_recv.at[x * 4 + place],
            device_id={"kv": q_target(n)},
            device_id_type=MESH,
        )

    def send_queries(n, carry):
        @pl.when(q_target(n) != me)
        def _():
            q_copy(n).start()

        @pl.when(q_target(n) == me)
        def _():
            pltpu.make_async_copy(q_out, q_place(), q_recv.at[x * 4 + place]).start()

        return carry

    lax.fori_loop(0, x_count * 4, send_queries, 0)
    for copy in own_copies():
        copy.start()
    arrived(blocks.at[1], block_sem.at[1])
    mask_columns(1)

    def o_target(slot, p):
        return slot * 8 + (core * 2 + p // 2) * 2 + p % 2

    def o_copies(i, p):
        slot = head_at(i)
        n = i * 4 + p
        return tuple(
            pltpu.make_async_remote_copy(
                src_ref=src.at[slot, p],
                dst_ref=dst.at[chip],
                send_sem=send.at[n],
                recv_sem=recv.at[chip],
                device_id={"kv": o_target(slot, p)},
                device_id_type=MESH,
            )
            for src, dst, send, recv in (
                (o_out, o_in, o_send, o_recv),
                (stat_out, stat_in, stat_send, stat_recv),
            )
        )

    def attend(i, carry):
        slot = head_at(i)
        for p in range(4):
            arrived(queries.at[slot, pl.ds(p * pair, pair)], q_recv.at[slot * 4 + p])
        for k, held in enumerate((keys, values)):
            arrived(held.at[slot, pl.ds(0, slots)], own_sem.at[i * 2 + k])
            arrived(held.at[slot, pl.ds(slots, slots)], kv_recv.at[i * 2 + k])
        query = jnp.concatenate([queries[slot], onehot[...]], axis=1)

        def scores_of(n):
            key = keys[slot, pl.ds(n * slots, slots)].reshape(span, HD)
            key = jnp.concatenate([key, bias[pl.ds(n * span, span), :]], axis=1)
            return dot(key, query, ((1,), (1,)))

        peak = jnp.full((8, wide), PEAK_FLOOR, F32)
        total = jnp.zeros((8, wide), F32)
        summed = jnp.zeros((HD, wide), F32)
        scores = scores_of(0)
        for n in range(2):
            coming = scores_of(1) if n == 0 else None
            scores = scores.reshape(span // 8, 8, wide)
            largest = jnp.max(jnp.max(scores, axis=0), axis=0, keepdims=True)
            new_peak = jnp.maximum(peak, largest)
            decay = jnp.exp2((peak - new_peak) * LOG2_SCALE)
            weights = jnp.exp2(scores * LOG2_SCALE - (new_peak * LOG2_SCALE)[None])
            total = total * decay + jnp.sum(weights, axis=0)
            weights = weights.reshape(span, wide).astype(BF16)
            value = values[slot, pl.ds(n * slots, slots)].reshape(span, HD)
            summed = summed * decay[0:1] + dot(value, weights, ((0,), (0,)))
            peak = new_peak
            scores = coming
        total = jnp.sum(total, axis=0, keepdims=True)
        for p in range(4):
            part = slice(p * pair, (p + 1) * pair)
            o_out[slot, p] = summed[:, part].astype(BF16)
            stat_out[slot, p] = jnp.concatenate(
                [peak[0:4, part], jnp.broadcast_to(total[:, part], (4, pair))], axis=0
            )
        for p in range(4):

            @pl.when(o_target(slot, p) != me)
            def _():
                for copy in o_copies(i, p):
                    copy.start()

            @pl.when(o_target(slot, p) == me)
            def _():
                pltpu.make_async_copy(o_out.at[slot, p], o_in.at[chip], o_recv.at[chip]).start()
                pltpu.make_async_copy(
                    stat_out.at[slot, p], stat_in.at[chip], stat_recv.at[chip]
                ).start()

        return carry

    lax.fori_loop(0, x_count, attend, 0)

    def await_sums(n, carry):
        arrived(o_in.at[n], o_recv.at[n])
        arrived(stat_in.at[n], stat_recv.at[n])
        return carry

    lax.fori_loop(0, chips, await_sums, 0)
    peaks = stat_in[:, 0, :]
    totals = stat_in[:, 4, :]
    share = jnp.exp2((peaks - jnp.max(peaks, axis=0, keepdims=True)) * LOG2_SCALE)
    share = share / jnp.sum(share * totals, axis=0, keepdims=True)
    joined = jnp.zeros((HD, pair), F32)
    for n in range(chips):
        joined = joined + share[n : n + 1] * o_in[n].astype(F32)
    joined = joined.T.astype(BF16)
    attended[core] = jnp.concatenate([joined[:rows], joined[rows:]], axis=1)
    share_heads = pltpu.make_async_remote_copy(
        src_ref=attended.at[core],
        dst_ref=attended.at[core],
        send_sem=att_sem.at[0],
        recv_sem=att_sem.at[1],
        device_id={"kv": sibling},
        device_id_type=MESH,
    )
    share_heads.start()

    def spread(count, first, q):
        at = lax.broadcasted_iota(I32, (count, rows), 0)
        row = (at // 16) * 4 + ((at // 8) % 2) * 2 + at % 2 + first
        hit = (row == lax.broadcasted_iota(I32, (count, rows), 1)) & ((at // 2) % 4 == q)
        return jnp.where(hit, 1.0, 0.0).astype(BF16)

    strip = min(512, lanes)

    def project(c):
        parts = [dot(spread(16 * chips, 0, q), attended[c]).astype(BF16) for q in range(4)]
        for n in range(lanes // strip):
            total = None
            for q in range(4):
                term = dot(parts[q], wo[c, :, pl.ds(q * lanes + n * strip, strip)])
                total = term if total is None else total + term
            yield pl.ds(n * strip, strip), total

    arrived(wo.at[core], own_sem.at[2 * x_count])
    for part, term in project(core):
        acc[:, part] = term
    arrived(wo.at[other], kv_recv.at[2 * x_count])
    arrived(attended.at[other], att_sem.at[1])
    for part, term in project(other):
        rs_out[:, :, part] = (acc[:, part] + term).astype(BF16).reshape(chips, 16, strip)

    def rs_copy(n):
        to = lax.rem(chip + n, chips)
        return pltpu.make_async_remote_copy(
            src_ref=rs_out.at[to],
            dst_ref=rs_in.at[chip],
            send_sem=rs_send.at[n],
            recv_sem=rs_recv.at[chip],
            device_id={"kv": to * 2 + core},
            device_id_type=MESH,
        )

    def send_terms(n, carry):
        rs_copy(n).start()
        return carry

    lax.fori_loop(1, chips, send_terms, 0)

    result = rs_out[chip].astype(F32)
    for q in range(4):
        own = hid[:, pl.ds(pl.multiple_of(core * half + q * lanes, lanes), lanes)]
        result = result + dot(spread(16, chip * 4, q), own)

    def add_term(n, total):
        source = lax.rem(chip + n, chips)
        arrived(rs_in.at[source], rs_recv.at[source])
        return total + rs_in[source].astype(F32)

    result = lax.fori_loop(1, chips, add_term, result)

    def fin_copy(c):
        return pltpu.make_async_remote_copy(
            src_ref=fin_out.at[c],
            dst_ref=fin_in.at[core],
            send_sem=fin_send.at[c],
            recv_sem=fin_recv.at[core],
            device_id={"section": after, "kv": chip * 2 + c},
            device_id_type=MESH,
        )

    for c in range(2):
        mine = result[8 * c : 8 * c + 8]
        fin_out[c] = jnp.concatenate(
            [mine[:, : lanes // 2], mine[:, lanes // 2 :]], axis=0
        ).astype(BF16)
        fin_copy(c).start()
    for c in range(2):
        arrived(fin_in.at[c], fin_recv.at[c])
    out[...] = fin_in[...]

    send_blocks.wait_send()
    for copy in swap_copies():
        copy.wait_send()

    def queries_left(n, carry):
        @pl.when(q_target(n) != me)
        def _():
            q_copy(n).wait_send()

        return carry

    lax.fori_loop(0, x_count * 4, queries_left, 0)

    def sums_left(i, carry):
        for p in range(4):

            @pl.when(o_target(head_at(i), p) != me)
            def _():
                for copy in o_copies(i, p):
                    copy.wait_send()

        return carry

    lax.fori_loop(0, x_count, sums_left, 0)
    share_heads.wait_send()

    def terms_left(n, carry):
        rs_copy(n).wait_send()
        return carry

    lax.fori_loop(1, chips, terms_left, 0)
    for c in range(2):
        fin_copy(c).wait_send()


def local(sections, kv_count, *args):
    hidden, _, query_weight, key_cache = args[:4]
    rows, width = hidden.shape[1:]
    slots, block = key_cache.shape[1:3]
    x_count, chips = kv_count // 8, kv_count // 2
    pair, wide = 2 * rows, 8 * rows
    lanes = width // 8
    dma = pltpu.SemaphoreType.DMA
    anywhere = pl.BlockSpec(memory_space=pl.ANY)
    scalars = pl.BlockSpec(memory_space=pltpu.SMEM)
    pieces = 4
    out = pl.pallas_call(
        functools.partial(kernel, sections, kv_count),
        out_shape=jax.ShapeDtypeStruct((2, 16, lanes // 2), BF16),
        in_specs=[anywhere] * 6 + [scalars] * 3,
        out_specs=pl.BlockSpec(memory_space=pltpu.VMEM),
        scratch_shapes=[
            pltpu.VMEM((rows, width), BF16),
            pltpu.VMEM((1, width), F32),
            pltpu.VMEM((width, 2 * HD), BF16),
            pltpu.VMEM((x_count, 2 * slots, block, HD), BF16),
            pltpu.VMEM((x_count, 2 * slots, block, HD), BF16),
            pltpu.VMEM((2, 2 * HD, width // 2), BF16),
            pltpu.VMEM((x_count, wide, HD), BF16),
            pltpu.VMEM((wide, 128), BF16),
            pltpu.VMEM((2 * slots * block, 128), BF16),
            pltpu.VMEM((2, 16, 128), F32),
            pltpu.VMEM((pair, HD), BF16),
            pltpu.VMEM((x_count, 4, HD, pair), BF16),
            pltpu.VMEM((x_count, 4, 8, pair), F32),
            pltpu.VMEM((chips, HD, pair), BF16),
            pltpu.VMEM((chips, 8, pair), F32),
            pltpu.VMEM((2, rows, 2 * HD), BF16),
            pltpu.VMEM((16 * chips, lanes), F32),
            pltpu.VMEM((chips, 16, lanes), BF16),
            pltpu.VMEM((chips, 16, lanes), BF16),
            pltpu.VMEM((2, 16, lanes // 2), BF16),
            pltpu.VMEM((2, 16, lanes // 2), BF16),
            dma((2,)),
            dma((pieces,)),
            dma((2 * x_count + 1,)),
            dma((2 * x_count + 1,)),
            dma((2 * x_count + 1,)),
            dma((2,)),
            dma((4 * x_count,)),
            dma((4 * x_count,)),
            dma((4 * x_count,)),
            dma((chips,)),
            dma((4 * x_count,)),
            dma((chips,)),
            dma((2,)),
            dma((chips,)),
            dma((chips,)),
            dma((2,)),
            dma((2,)),
        ],
        compiler_params=pltpu.CompilerParams(
            collective_id=0, has_side_effects=True, vmem_limit_bytes=60 << 20
        ),
        name="relay_attention",
    )(*args)
    out = out.reshape(2, 2, 4, 2, lanes // 2).transpose(3, 0, 2, 1, 4)
    return out.reshape(1, 2, width)


def solution(mesh):
    placed = (
        P("section", None, None),
        P("section", None),
        P("section", None, "kv"),
        P("section", "kv", None, None),
        P("section", "kv", None, None),
        P("section", "kv", None),
        P("kv"),
        P(),
        P(),
    )
    sections, kv_count = mesh.shape["section"], mesh.shape["kv"]
    return jax.shard_map(
        functools.partial(local, sections, kv_count),
        mesh=mesh,
        in_specs=placed,
        out_specs=P("section", "kv", None),
        check_vma=False,
    )
```

time: 638 us -> 58.3 us (0.09)
  waiting for transfers between devices: 291 us -> 0 us
  other arithmetic: 128 us -> 0 us
  local copies, waits for them, and re-layouts: 85.6 us -> 1.44 us
  matrix products: 63.1 us -> 0 us
  Pallas kernels: 0 us -> 56 us
  blocking collectives: 49.5 us -> 0 us
  between operations: 14 us -> 0.67 us
    all_gather x2 -> x0, waiting for transfers between devices: 185 us -> none  [the longest x1 153 us: merged(): pieces = jax.tree.map(lambda part: lax.all_gather(part, axis), value)]
    add x64 -> x0, other arithmetic: 108 us -> none  [the longest x31 82.8 us: join_partials(): sums_a * weight_a[..., None] + sums_b * weight_b[..., None]]
    psum x1 -> x0, waiting for transfers between devices: 103 us -> none  [local(): whole_sum = lax.psum(term.astype(jnp.bfloat16), 'kv').astype(jnp.float32)]
    dot_general x18 -> x0, matrix products: 63.1 us -> none  [the longest x8 31.7 us: per_head(): jnp.einsum('rgc,cd->rgd', weights.astype(jnp.bfloat16), value_head, prefe...]
    pallas_call x0 -> x1, Pallas kernels: none -> 56 us  [local(): pl.pallas_call(functools.partial(kernel, sections, kv_count), out_shape=j...]
    all_gather x2 -> x0, blocking collectives: 49.5 us -> none  [merged(): pieces = jax.tree.map(lambda part: lax.all_gather(part, axis), value)]
    slice x3 -> x0, local copies, waits for them, and re-layouts: 43.7 us -> none  [merged(): tail = jax.tree.map(lambda part: part[1:], pieces)]
    while x16 -> x0, local copies, waits for them, and re-layouts: 20.6 us -> none
  transfers between devices with their start and end apart: 4 -> 0, of which waited for: 4 -> 0; matrix products, arithmetic and copies ran while one was open for 2% -> 0% of each run, Pallas kernels for 0% -> 0%
where the time goes in v1:
time: 58.3 us; the launch traced here: 58.1 us
  Pallas kernels  56 us (96%)
  local copies, waits for them, and re-layouts  1.44 us (2%)
  between operations  0.67 us (1%)
    pallas_call x1, Pallas kernels, local(): pl.pallas_call(functools.partial(kernel, sections, kv_count), out_shape=j...  56 us

profile of v1, /device:TPU:1, one launch (start us, length us, event | category | flops | bytes accessed | tf_op | source)
XLA Modules:
  0.0 58.1 jit_solution(13425316635980578653)
XLA Ops:
  0.7 56.0 %relay_attention.1 = bf16[2,16,512]{2,1,0:T(8,128)(2,1)} custom-call(bf16[1,64,8192]{2,1,0:T(8,128)(2,1)} %hid_h.1, f32[1,8192]{1,0:T(1,128)} %gain_h.1, bf16[1,8192,256]{2,1,0:T(8,128)(2,1)} %wq_h.1, bf16[1,12,256,1024]{3,2,1,0:T(8,128)(2,1)} %key_h.1, bf16[1,12,256,1024]{3,2,1,0:T(8,128)(2,1)} %value_h.1, bf16[1,256,8192]{2,1,0:T(8,128)(2,1)} %wo_h.1, ...), custom_call_target="tpu_custom_call" | custom-call | tf_op jit(solution)/shard_map/relay_attention/pallas_call | solution.py:508
  56.7 0.8 %reshape.6 = bf16[2,2,4,2,512]{4,3,2,1,0:T(2,128)(2,1)S(1)} reshape(bf16[2,16,512]{2,1,0:T(8,128)(2,1)} %relay_attention.1) | data formatting | bytes 65536 | tf_op jit(solution)/shard_map/reshape | solution.py:558
  57.5 0.6 %reshape.7 = bf16[1,2,8192]{2,1,0:T(2,128)(2,1)} reshape(bf16[2,2,4,2,512]{4,3,2,1,0:T(2,128)(2,1)S(1)} %copy.10) | data formatting | bytes 65536 | tf_op jit(solution)/shard_map/reshape | solution.py:559
  (1 shorter events, 0.0 us)

commit v2 on v1

v2 whole, which is shorter than its diff:
```python
import functools
import math

import jax
import jax.numpy as jnp
from jax import lax
from jax.experimental import pallas as pl
from jax.experimental.pallas import tpu as pltpu
from jax.sharding import PartitionSpec as P

HD = 128
LOG2_SCALE = math.log2(math.e) / math.sqrt(HD)
HIDDEN_BY_MASK = -1e30
PEAK_FLOOR = -1e28
MESH = pl.DeviceIdType.MESH
BF16, F32, I32 = jnp.bfloat16, jnp.float32, jnp.int32


def dot(a, b, contract=((1,), (0,))):
    return lax.dot_general(a, b, (contract, ((), ())), preferred_element_type=F32)


def arrived(ref, sem):
    pltpu.make_async_copy(ref, ref, sem).wait()


def kernel(
    sections,
    kv_count,
    hid_h,
    gain_h,
    wq_h,
    key_h,
    value_h,
    wo_h,
    block_pos_h,
    lengths_h,
    span_start_h,
    out,
    block_pos,
    lengths,
    span_start,
    hid,
    gain,
    wq,
    keys,
    values,
    wo,
    queries,
    onehot,
    bias,
    blocks,
    scores,
    q_out,
    o_out,
    stat_out,
    o_in,
    stat_in,
    attended,
    acc,
    rs_out,
    rs_in,
    fin_out,
    fin_in,
    in_sem,
    wq_sem,
    own_sem,
    kv_send,
    kv_recv,
    block_sem,
    q_send,
    q_recv,
    o_send,
    o_recv,
    stat_send,
    stat_recv,
    att_sem,
    rs_send,
    rs_recv,
    fin_send,
    fin_recv,
):
    rows, width = hid.shape
    x_count = kv_count // 8
    chips = kv_count // 2
    slots, block = key_h.shape[1], key_h.shape[2]
    half = width // 2
    lanes = rs_out.shape[2]
    strips = rs_send.shape[0]
    strip = lanes // strips
    span = slots * block
    wide = onehot.shape[0]
    pair = 2 * rows
    section = lax.axis_index("section")
    me = lax.axis_index("kv")
    chip = lax.div(me, 2)
    core = lax.rem(me, 2)
    other = 1 - core
    sibling = chip * 2 + other
    x = lax.div(chip, 4)
    z = lax.rem(chip, 4)
    side = lax.div(z, 2)
    place = core * 2 + lax.rem(z, 2)

    load_hid = pltpu.make_async_copy(hid_h.at[0], hid, in_sem.at[0])
    load_gain = pltpu.make_async_copy(gain_h, gain, in_sem.at[1])
    load_hid.start()
    load_gain.start()
    pieces = wq_sem.shape[0]
    deep = wq.shape[0] // pieces

    def load_wq(n):
        part = pl.ds(n * deep, deep)
        return pltpu.make_async_copy(wq_h.at[0, part], wq.at[part], wq_sem.at[n])

    for n in range(pieces):
        load_wq(n).start()
    scalar_loads = [
        pltpu.make_async_copy(src, dst, in_sem.at[2 + n])
        for n, (src, dst) in enumerate(
            ((block_pos_h, block_pos), (lengths_h, lengths), (span_start_h, span_start))
        )
    ]
    for load in scalar_loads:
        load.start()

    barrier = pltpu.get_barrier_semaphore()

    def greet(n, carry):
        @pl.when(n != me)
        def _():
            pl.semaphore_signal(barrier, inc=1, device_id={"kv": n}, device_id_type=MESH)

        return carry

    lax.fori_loop(0, kv_count, greet, 0)
    after = lax.rem(section + 1, sections)
    before = lax.rem(section + sections - 1, sections)
    for there in (after, before):
        for c in range(2):
            pl.semaphore_signal(
                barrier,
                inc=1,
                device_id={"section": there, "kv": chip * 2 + c},
                device_id_type=MESH,
            )

    load_hid.wait()
    load_gain.wait()
    step = min(1024, deep)
    squares = jnp.zeros((rows, 1), F32)
    for n in range(width // step):
        part = hid[:, n * step : (n + 1) * step].astype(F32)
        squares = squares + jnp.sum(part * part, axis=1, keepdims=True)
    scale = lax.rsqrt(squares / width + 1e-05)
    projected = jnp.zeros((rows, 2 * HD), F32)
    for n in range(width // step):
        if n * step % deep == 0:
            load_wq(n * step // deep).wait()
        part = pl.ds(n * step, step)
        normed = (hid[:, part].astype(F32) * scale * gain[:, part]).astype(BF16)
        projected = projected + dot(normed, wq[part, :])
    projected = projected * LOG2_SCALE
    q_out[pl.ds(0, rows), :] = projected[:, :HD].astype(BF16)
    q_out[pl.ds(rows, rows), :] = projected[:, HD:].astype(BF16)

    def moved(i, at_z):
        return lax.rem((i + 1) * jnp.where(lax.rem(at_z, 2) == 0, 1, x_count - 1), x_count)

    def head_at(i):
        return lax.rem(x + moved(i, z), x_count)

    def head_lanes(slot, c):
        return pl.ds(pl.multiple_of((slot * 2 + c) * HD, HD), HD)

    def own_copies():
        copies = []
        for i in range(x_count):
            slot = head_at(i)
            for k, (src, dst) in enumerate(((key_h, keys), (value_h, values))):
                copies.append(
                    pltpu.make_async_copy(
                        src.at[0, :, :, head_lanes(slot, core)],
                        dst.at[slot, pl.ds(0, slots)],
                        own_sem.at[i * 2 + k],
                    )
                )
        copies.append(
            pltpu.make_async_copy(
                wo_h.at[0, :, pl.ds(pl.multiple_of(core * half, half), half)],
                wo.at[core],
                own_sem.at[2 * x_count],
            )
        )
        return copies

    def to_sibling(src, dst, n):
        return pltpu.make_async_remote_copy(
            src_ref=src,
            dst_ref=dst,
            send_sem=kv_send.at[n],
            recv_sem=kv_recv.at[n],
            device_id={"kv": sibling},
            device_id_type=MESH,
        )

    def swap_copies():
        copies = []
        for i in range(x_count):
            slot = head_at(i)
            for k, (src, dst) in enumerate(((key_h, keys), (value_h, values))):
                copies.append(
                    to_sibling(
                        src.at[0, :, :, head_lanes(slot, other)],
                        dst.at[slot, pl.ds(slots, slots)],
                        i * 2 + k,
                    )
                )
        copies.append(
            to_sibling(
                wo_h.at[0, :, pl.ds(pl.multiple_of(other * half, half), half)],
                wo.at[core],
                2 * x_count,
            )
        )
        return copies

    for copy in own_copies():
        copy.start()
    pl.semaphore_wait(barrier, kv_count - 1 + 4)

    def q_target(n):
        to_z = lax.rem(z + n, 4)
        to_x = lax.rem(x + x_count - moved(lax.div(n, 4), to_z), x_count)
        return to_x * 8 + to_z * 2 + side

    def q_place():
        return queries.at[x, pl.ds(pl.multiple_of(place * pair, pair), pair)]

    def q_copy(n):
        return pltpu.make_async_remote_copy(
            src_ref=q_out,
            dst_ref=q_place(),
            send_sem=q_send.at[n],
            recv_sem=q_recv.at[x * 4 + place],
            device_id={"kv": q_target(n)},
            device_id_type=MESH,
        )

    def send_queries(n, carry):
        @pl.when(q_target(n) != me)
        def _():
            q_copy(n).start()

        @pl.when(q_target(n) == me)
        def _():
            pltpu.make_async_copy(q_out, q_place(), q_recv.at[x * 4 + place]).start()

        return carry

    lax.fori_loop(0, 4, send_queries, 0)

    for load in scalar_loads:
        load.wait()
    blocks[0] = jnp.zeros((16, 128), F32)
    for j in range(slots):
        blocks[0, j : j + 1, :] = jnp.full((1, 128), block_pos[j], I32).astype(F32)
    send_blocks = pltpu.make_async_remote_copy(
        src_ref=blocks.at[0],
        dst_ref=blocks.at[1],
        send_sem=block_sem.at[0],
        recv_sem=block_sem.at[1],
        device_id={"kv": sibling},
        device_id_type=MESH,
    )
    send_blocks.start()
    for copy in swap_copies():
        copy.start()
    lane = lax.broadcasted_iota(I32, (1, 128), 1)
    prefill = rows - lengths.shape[0]
    limits = span_start[0] + lane + 1
    for r in range(lengths.shape[0]):
        limits = jnp.where(lane == prefill + r, lengths[r], limits)
    limits = limits.astype(F32)
    token = lax.broadcasted_iota(I32, (block, 128), 0).astype(F32)

    def mask_columns(which):
        for j in range(slots):
            position = blocks[which, j : j + 1, :] * float(block) + token
            bias[pl.ds((which * slots + j) * block, block), :] = jnp.where(
                position < limits, 0.0, HIDDEN_BY_MASK
            ).astype(BF16)

    mask_columns(0)
    onehot[...] = jnp.where(
        lax.rem(lax.broadcasted_iota(I32, (wide, 128), 0), rows)
        == lax.broadcasted_iota(I32, (wide, 128), 1),
        1.0,
        0.0,
    ).astype(BF16)
    arrived(blocks.at[1], block_sem.at[1])
    mask_columns(1)
    if x_count > 1:
        lax.fori_loop(4, 8, send_queries, 0)

    def o_target(slot, p):
        return slot * 8 + (core * 2 + p % 2) * 2 + p // 2

    def o_copies(i, p):
        slot = head_at(i)
        n = i * 4 + p
        return tuple(
            pltpu.make_async_remote_copy(
                src_ref=src.at[slot, p],
                dst_ref=dst.at[chip],
                send_sem=send.at[n],
                recv_sem=recv.at[chip],
                device_id={"kv": o_target(slot, p)},
                device_id_type=MESH,
            )
            for src, dst, send, recv in (
                (o_out, o_in, o_send, o_recv),
                (stat_out, stat_in, stat_send, stat_recv),
            )
        )

    def await_first(i):
        slot = head_at(i)
        for p in range(4):
            arrived(queries.at[slot, pl.ds(p * pair, pair)], q_recv.at[slot * 4 + p])
        arrived(keys.at[slot, pl.ds(0, slots)], own_sem.at[i * 2])

    def score(i, n):
        slot = head_at(i)
        query = jnp.concatenate([queries[slot], onehot[...]], axis=1)
        key = keys[slot, pl.ds(n * slots, slots)].reshape(span, HD)
        key = jnp.concatenate([key, bias[pl.ds(n * span, span), :]], axis=1)
        scores[n] = dot(key, query, ((1,), (1,)))

    def weigh(i, n, state, columns):
        peak, total, summed = state
        part = scores[n, :, columns].reshape(span // 8, 8, peak.shape[1])
        largest = jnp.max(jnp.max(part, axis=0), axis=0, keepdims=True)
        new_peak = jnp.maximum(peak, largest)
        decay = jnp.exp2(peak - new_peak)
        weights = jnp.exp2(part - new_peak[None])
        total = total * decay + jnp.sum(weights, axis=0)
        weights = weights.reshape(span, peak.shape[1]).astype(BF16)
        value = values[head_at(i), pl.ds(n * slots, slots)].reshape(span, HD)
        summed = summed * decay[0:1] + dot(value, weights, ((0,), (0,)))
        return new_peak, total, summed

    def attend(i, last):
        slot = head_at(i)
        arrived(values.at[slot, pl.ds(0, slots)], own_sem.at[i * 2 + 1])
        arrived(keys.at[slot, pl.ds(slots, slots)], kv_recv.at[i * 2])
        score(i, 1)
        state = (
            jnp.full((8, wide), PEAK_FLOOR, F32),
            jnp.zeros((8, wide), F32),
            jnp.zeros((HD, wide), F32),
        )
        state = weigh(i, 0, state, pl.ds(0, wide))
        arrived(values.at[slot, pl.ds(slots, slots)], kv_recv.at[i * 2 + 1])
        if not last:
            await_first(i + 1)
            score(i + 1, 0)
        cuts = 2 if last else 1
        for cut in range(cuts):
            size = wide // cuts
            columns = slice(cut * size, (cut + 1) * size)
            peak, total, summed = weigh(
                i, 1, [value[:, columns] for value in state], pl.ds(cut * size, size)
            )
            total = jnp.sum(total, axis=0, keepdims=True)
            owners = range(cut * 4 // cuts, (cut + 1) * 4 // cuts)
            for p in owners:
                part = slice(p * pair - cut * size, (p + 1) * pair - cut * size)
                o_out[slot, p] = summed[:, part].astype(BF16)
                stat_out[slot, p] = jnp.concatenate(
                    [peak[0:4, part], jnp.broadcast_to(total[:, part], (4, pair))], axis=0
                )
            for p in owners:

                @pl.when(o_target(slot, p) != me)
                def _():
                    for copy in o_copies(i, p):
                        copy.start()

                @pl.when(o_target(slot, p) == me)
                def _():
                    pltpu.make_async_copy(
                        o_out.at[slot, p], o_in.at[chip], o_recv.at[chip]
                    ).start()
                    pltpu.make_async_copy(
                        stat_out.at[slot, p], stat_in.at[chip], stat_recv.at[chip]
                    ).start()

    def attend_inner(i, carry):
        attend(i, False)
        return carry

    await_first(0)
    score(0, 0)
    if x_count > 2:
        lax.fori_loop(8, x_count * 4, send_queries, 0)
    lax.fori_loop(0, x_count - 1, attend_inner, 0)
    attend(x_count - 1, True)

    def queries_left(n, carry):
        @pl.when(q_target(n) != me)
        def _():
            q_copy(n).wait_send()

        return carry

    lax.fori_loop(0, x_count * 4, queries_left, 0)
    send_blocks.wait_send()
    for copy in swap_copies():
        copy.wait_send()

    def join(state, columns):
        peak, total, summed = state
        sources = [lax.rem(x + k, x_count) * 4 + at_z for k in columns for at_z in range(4)]
        for source in sources:
            arrived(stat_in.at[source], stat_recv.at[source])
            arrived(o_in.at[source], o_recv.at[source])
        stats = [stat_in[source] for source in sources]
        new_peak = functools.reduce(jnp.maximum, [stat[0:1] for stat in stats], peak)
        decay = jnp.exp2(peak - new_peak)
        total, summed = total * decay, summed * decay
        for source, stat in zip(sources, stats):
            share = jnp.exp2(stat[0:1] - new_peak)
            total = total + share * stat[4:5]
            summed = summed + share * o_in[source].astype(F32)
        return new_peak, total, summed

    state = (
        jnp.full((1, pair), PEAK_FLOOR, F32),
        jnp.zeros((1, pair), F32),
        jnp.zeros((HD, pair), F32),
    )
    if x_count > 1:
        state = join(state, range(1, x_count))
    _, total, summed = join(state, range(1))
    joined = (summed / total).T.astype(BF16)
    attended[core] = jnp.concatenate([joined[:rows], joined[rows:]], axis=1)
    share_heads = pltpu.make_async_remote_copy(
        src_ref=attended.at[core],
        dst_ref=attended.at[core],
        send_sem=att_sem.at[0],
        recv_sem=att_sem.at[1],
        device_id={"kv": sibling},
        device_id_type=MESH,
    )
    share_heads.start()

    def spread(count, first, q):
        at = lax.broadcasted_iota(I32, (count, rows), 0)
        row = (at // 16) * 4 + ((at // 8) % 2) * 2 + at % 2 + first
        hit = (row == lax.broadcasted_iota(I32, (count, rows), 1)) & ((at // 2) % 4 == q)
        return jnp.where(hit, 1.0, 0.0).astype(BF16)

    def spread_heads(c):
        return [dot(spread(16 * chips, 0, q), attended[c]).astype(BF16) for q in range(4)]

    def project(c, parts, n):
        total = None
        for q in range(4):
            term = dot(parts[q], wo[c, :, pl.ds(q * lanes + n * strip, strip)])
            total = term if total is None else total + term
        return total

    steps = sorted(
        ((a, b) for a in range(x_count) for b in range(4) if (a, b) != (0, 0)),
        key=lambda ab: -min(ab[0], x_count - ab[0]) - min(ab[1], 4 - ab[1]),
    )

    def chip_at(n):
        return lax.rem(x + steps[n][0], x_count) * 4 + lax.rem(z + steps[n][1], 4)

    def rs_copy(n, k):
        to = chip_at(n)
        part = pl.ds(k * strip, strip)
        return pltpu.make_async_remote_copy(
            src_ref=rs_out.at[to, :, part],
            dst_ref=rs_in.at[chip, :, part],
            send_sem=rs_send.at[k, n],
            recv_sem=rs_recv.at[k, chip],
            device_id={"kv": to * 2 + core},
            device_id_type=MESH,
        )

    arrived(wo.at[core], own_sem.at[2 * x_count])
    parts = spread_heads(core)
    for k in range(strips):
        acc[:, pl.ds(k * strip, strip)] = project(core, parts, k)
    arrived(wo.at[other], kv_recv.at[2 * x_count])
    arrived(attended.at[other], att_sem.at[1])
    parts = spread_heads(other)
    for k in range(strips):
        part = pl.ds(k * strip, strip)
        term = acc[:, part] + project(other, parts, k)
        rs_out[:, :, part] = term.astype(BF16).reshape(chips, 16, strip)

        for n in range(len(steps)):
            rs_copy(n, k).start()

    def sums_left(i, carry):
        for p in range(4):

            @pl.when(o_target(head_at(i), p) != me)
            def _():
                for copy in o_copies(i, p):
                    copy.wait_send()

        return carry

    lax.fori_loop(0, x_count, sums_left, 0)
    share_heads.wait_send()

    results = []
    for k in range(strips):
        part = pl.ds(k * strip, strip)
        result = rs_out[chip, :, part].astype(F32)
        for q in range(4):
            start = core * half + q * lanes + k * strip
            own = hid[:, pl.ds(pl.multiple_of(start, strip), strip)]
            result = result + dot(spread(16, chip * 4, q), own)
        results.append(result)
    for k in range(strips):
        part = pl.ds(k * strip, strip)

        for n in reversed(range(len(steps))):
            source = chip_at(n)
            arrived(rs_in.at[source, :, part], rs_recv.at[k, source])
            results[k] = results[k] + rs_in[source, :, part].astype(F32)
    result = jnp.concatenate(results, axis=1)

    def fin_copy(c):
        return pltpu.make_async_remote_copy(
            src_ref=fin_out.at[c],
            dst_ref=fin_in.at[core],
            send_sem=fin_send.at[c],
            recv_sem=fin_recv.at[core],
            device_id={"section": after, "kv": chip * 2 + c},
            device_id_type=MESH,
        )

    for c in range(2):
        mine = result[8 * c : 8 * c + 8]
        fin_out[c] = jnp.concatenate(
            [mine[:, : lanes // 2], mine[:, lanes // 2 :]], axis=0
        ).astype(BF16)
        fin_copy(c).start()

    for k in range(strips):
        for n in range(len(steps)):
            rs_copy(n, k).wait_send()
    for c in range(2):
        arrived(fin_in.at[c], fin_recv.at[c])
    final = []
    for c in range(2):
        rows_in = fin_in[c].astype(F32)
        for q in range(4):
            for h in range(2):
                final.append(rows_in[h * 8 + q * 2 : h * 8 + q * 2 + 2])
    out[0] = jnp.concatenate(final, axis=1)
    for c in range(2):
        fin_copy(c).wait_send()


def local(sections, kv_count, *args):
    hidden, _, query_weight, key_cache = args[:4]
    rows, width = hidden.shape[1:]
    slots, block = key_cache.shape[1:3]
    x_count, chips = kv_count // 8, kv_count // 2
    pair, wide = 2 * rows, 8 * rows
    lanes = width // 8
    strips = 2
    pieces = 4
    dma = pltpu.SemaphoreType.DMA
    out = pl.pallas_call(
        functools.partial(kernel, sections, kv_count),
        out_shape=pltpu.VMEM((1, 2, width), F32),
        in_specs=[pl.BlockSpec(memory_space=pl.ANY)] * 9,
        out_specs=pl.BlockSpec(memory_space=pltpu.VMEM),
        scratch_shapes=[
            pltpu.SMEM(args[6].shape, I32),
            pltpu.SMEM(args[7].shape, I32),
            pltpu.SMEM(args[8].shape, I32),
            pltpu.VMEM((rows, width), BF16),
            pltpu.VMEM((1, width), F32),
            pltpu.VMEM((width, 2 * HD), BF16),
            pltpu.VMEM((x_count, 2 * slots, block, HD), BF16),
            pltpu.VMEM((x_count, 2 * slots, block, HD), BF16),
            pltpu.VMEM((2, 2 * HD, width // 2), BF16),
            pltpu.VMEM((x_count, wide, HD), BF16),
            pltpu.VMEM((wide, 128), BF16),
            pltpu.VMEM((2 * slots * block, 128), BF16),
            pltpu.VMEM((2, 16, 128), F32),
            pltpu.VMEM((2, slots * block, wide), F32),
            pltpu.VMEM((pair, HD), BF16),
            pltpu.VMEM((x_count, 4, HD, pair), BF16),
            pltpu.VMEM((x_count, 4, 8, pair), F32),
            pltpu.VMEM((chips, HD, pair), BF16),
            pltpu.VMEM((chips, 8, pair), F32),
            pltpu.VMEM((2, rows, 2 * HD), BF16),
            pltpu.VMEM((16 * chips, lanes), F32),
            pltpu.VMEM((chips, 16, lanes), BF16),
            pltpu.VMEM((chips, 16, lanes), BF16),
            pltpu.VMEM((2, 16, lanes // 2), BF16),
            pltpu.VMEM((2, 16, lanes // 2), BF16),
            dma((5,)),
            dma((pieces,)),
            dma((2 * x_count + 1,)),
            dma((2 * x_count + 1,)),
            dma((2 * x_count + 1,)),
            dma((2,)),
            dma((4 * x_count,)),
            dma((4 * x_count,)),
            dma((4 * x_count,)),
            dma((chips,)),
            dma((4 * x_count,)),
            dma((chips,)),
            dma((2,)),
            dma((strips, chips)),
            dma((strips, chips)),
            dma((2,)),
            dma((2,)),
        ],
        compiler_params=pltpu.CompilerParams(
            collective_id=0, has_side_effects=True, vmem_limit_bytes=60 << 20
        ),
        name="relay_attention",
    )(*args)
    return out.astype(BF16)


def solution(mesh):
    placed = (
        P("section", None, None),
        P("section", None),
        P("section", None, "kv"),
        P("section", "kv", None, None),
        P("section", "kv", None, None),
        P("section", "kv", None),
        P("kv"),
        P(),
        P(),
    )
    sections, kv_count = mesh.shape["section"], mesh.shape["kv"]
    return jax.shard_map(
        functools.partial(local, sections, kv_count),
        mesh=mesh,
        in_specs=placed,
        out_specs=P("section", "kv", None),
        check_vma=False,
    )
```

time: 58.3 us -> 53 us (0.909)
  Pallas kernels: 56 us -> 51.6 us
  local copies, waits for them, and re-layouts: 1.44 us -> 0 us
  other arithmetic: 0 us -> 0.64 us
    pallas_call x1, Pallas kernels: 56 us -> 51.6 us  [local(): pl.pallas_call(functools.partial(kernel, sections, kv_count), out_shape=p...]
    reshape x2 -> x0, local copies, waits for them, and re-layouts: 1.42 us -> none  [the longest x1 0.78 us: local(): out = out.reshape(2, 2, 4, 2, lanes // 2).transpose(3, 0, 2, 1, 4)]
    convert_element_type x0 -> x1, other arithmetic: none -> 0.64 us  [local(): return out.astype(BF16)]
where the time goes in v2:
time: 53 us; the launch traced here: 52.9 us
  Pallas kernels  51.6 us (97%)
  between operations  0.66 us (1%)
  other arithmetic  0.64 us (1%)
    pallas_call x1, Pallas kernels, local(): pl.pallas_call(functools.partial(kernel, sections, kv_count), out_shape=p...  51.6 us

profile of v2, /device:TPU:1, one launch (start us, length us, event | category | flops | bytes accessed | tf_op | source)
XLA Modules:
  0.0 52.9 jit_solution(16577127914031140693)
XLA Ops:
  0.7 51.6 %relay_attention.1 = f32[1,2,8192]{2,1,0:T(2,128)S(1)} custom-call(bf16[1,64,8192]{2,1,0:T(8,128)(2,1)} %hid_h.1, f32[1,8192]{1,0:T(1,128)} %gain_h.1, bf16[1,8192,256]{2,1,0:T(8,128)(2,1)} %wq_h.1, bf16[1,12,256,1024]{3,2,1,0:T(8,128)(2,1)} %key_h.1, bf16[1,12,256,1024]{3,2,1,0:T(8,128)(2,1)} %value_h.1, bf16[1,256,8192]{2,1,0:T(8,128)(2,1)} %wo_h.1, ...), custom_call_target="tpu_custom_call" | custom-call | tf_op jit(solution)/shard_map/relay_attention/pallas_call | solution.py:583
  52.3 0.6 %convert_element_type.3 = bf16[1,2,8192]{2,1,0:T(2,128)(2,1)} convert(f32[1,2,8192]{2,1,0:T(2,128)S(1)} %relay_attention.1) | non-fusion elementwise | flops 16384 | bytes 98304 | tf_op jit(solution)/shard_map/convert_element_type | solution.py:637

commit v3 on v2

--- a/solution.py
+++ b/solution.py
@@ -86,8 +86,8 @@
     slots, block = key_h.shape[1], key_h.shape[2]
     half = width // 2
     lanes = rs_out.shape[2]
-    strips = rs_send.shape[0]
-    strip = lanes // strips
+    strip = min(512, lanes)
+    strips = lanes // strip
     span = slots * block
     wide = onehot.shape[0]
     pair = 2 * rows
@@ -194,11 +194,11 @@
         )
         return copies
 
-    def to_sibling(src, dst, n):
+    def to_sibling(src, dst, n, kind):
         return pltpu.make_async_remote_copy(
             src_ref=src,
             dst_ref=dst,
-            send_sem=kv_send.at[n],
+            send_sem=kv_send.at[kind],
             recv_sem=kv_recv.at[n],
             device_id={"kv": sibling},
             device_id_type=MESH,
@@ -214,6 +214,7 @@
                         src.at[0, :, :, head_lanes(slot, other)],
                         dst.at[slot, pl.ds(slots, slots)],
                         i * 2 + k,
+                        k,
                     )
                 )
         copies.append(
@@ -221,6 +222,7 @@
                 wo_h.at[0, :, pl.ds(pl.multiple_of(other * half, half), half)],
                 wo.at[core],
                 2 * x_count,
+                2,
             )
         )
         return copies
@@ -241,8 +243,8 @@
         return pltpu.make_async_remote_copy(
             src_ref=q_out,
             dst_ref=q_place(),
-            send_sem=q_send.at[n],
-            recv_sem=q_recv.at[x * 4 + place],
+            send_sem=q_send,
+            recv_sem=q_recv.at[x],
             device_id={"kv": q_target(n)},
             device_id_type=MESH,
         )
@@ -254,7 +256,7 @@
 
         @pl.when(q_target(n) == me)
         def _():
-            pltpu.make_async_copy(q_out, q_place(), q_recv.at[x * 4 + place]).start()
+            pltpu.make_async_copy(q_out, q_place(), q_recv.at[x]).start()
 
         return carry
 
@@ -306,15 +308,17 @@
     def o_target(slot, p):
         return slot * 8 + (core * 2 + p % 2) * 2 + p // 2
 
+    def column_of(i):
+        return jnp.where(i == x_count - 1, 1, 0)
+
     def o_copies(i, p):
         slot = head_at(i)
-        n = i * 4 + p
         return tuple(
             pltpu.make_async_remote_copy(
                 src_ref=src.at[slot, p],
                 dst_ref=dst.at[chip],
-                send_sem=send.at[n],
-                recv_sem=recv.at[chip],
+                send_sem=send,
+                recv_sem=recv.at[column_of(i)],
                 device_id={"kv": o_target(slot, p)},
                 device_id_type=MESH,
             )
@@ -326,8 +330,7 @@
 
     def await_first(i):
         slot = head_at(i)
-        for p in range(4):
-            arrived(queries.at[slot, pl.ds(p * pair, pair)], q_recv.at[slot * 4 + p])
+        arrived(queries.at[slot], q_recv.at[slot])
         arrived(keys.at[slot, pl.ds(0, slots)], own_sem.at[i * 2])
 
     def score(i, n):
@@ -390,10 +393,10 @@
                 @pl.when(o_target(slot, p) == me)
                 def _():
                     pltpu.make_async_copy(
-                        o_out.at[slot, p], o_in.at[chip], o_recv.at[chip]
+                        o_out.at[slot, p], o_in.at[chip], o_recv.at[column_of(i)]
                     ).start()
                     pltpu.make_async_copy(
-                        stat_out.at[slot, p], stat_in.at[chip], stat_recv.at[chip]
+                        stat_out.at[slot, p], stat_in.at[chip], stat_recv.at[column_of(i)]
                     ).start()
 
     def attend_inner(i, carry):
@@ -407,24 +410,27 @@
     lax.fori_loop(0, x_count - 1, attend_inner, 0)
     attend(x_count - 1, True)
 
-    def queries_left(n, carry):
-        @pl.when(q_target(n) != me)
+    def left(ref, sem):
+        @pl.when(side == core)
         def _():
-            q_copy(n).wait_send()
-
-        return carry
-
-    lax.fori_loop(0, x_count * 4, queries_left, 0)
+            arrived(ref.at[pl.ds(0, chips - 1)], sem)
+
+        @pl.when(side != core)
+        def _():
+            arrived(ref, sem)
+
+    left(o_in, q_send)
     send_blocks.wait_send()
-    for copy in swap_copies():
-        copy.wait_send()
+    arrived(keys.at[:, pl.ds(slots, slots)], kv_send.at[0])
+    arrived(values.at[:, pl.ds(slots, slots)], kv_send.at[1])
+    arrived(wo.at[core], kv_send.at[2])
 
     def join(state, columns):
         peak, total, summed = state
         sources = [lax.rem(x + k, x_count) * 4 + at_z for k in columns for at_z in range(4)]
-        for source in sources:
-            arrived(stat_in.at[source], stat_recv.at[source])
-            arrived(o_in.at[source], o_recv.at[source])
+        which = 1 if 0 in columns else 0
+        arrived(stat_in.at[pl.ds(0, len(sources))], stat_recv.at[which])
+        arrived(o_in.at[pl.ds(0, len(sources))], o_recv.at[which])
         stats = [stat_in[source] for source in sources]
         new_peak = functools.reduce(jnp.maximum, [stat[0:1] for stat in stats], peak)
         decay = jnp.exp2(peak - new_peak)
@@ -479,14 +485,13 @@
     def chip_at(n):
         return lax.rem(x + steps[n][0], x_count) * 4 + lax.rem(z + steps[n][1], 4)
 
-    def rs_copy(n, k):
+    def rs_copy(n):
         to = chip_at(n)
-        part = pl.ds(k * strip, strip)
         return pltpu.make_async_remote_copy(
-            src_ref=rs_out.at[to, :, part],
-            dst_ref=rs_in.at[chip, :, part],
-            send_sem=rs_send.at[k, n],
-            recv_sem=rs_recv.at[k, chip],
+            src_ref=rs_out.at[to],
+            dst_ref=rs_in.at[chip],
+            send_sem=rs_send,
+            recv_sem=rs_recv,
             device_id={"kv": to * 2 + core},
             device_id_type=MESH,
         )
@@ -502,21 +507,11 @@
         part = pl.ds(k * strip, strip)
         term = acc[:, part] + project(other, parts, k)
         rs_out[:, :, part] = term.astype(BF16).reshape(chips, 16, strip)
-
-        for n in range(len(steps)):
-            rs_copy(n, k).start()
-
-    def sums_left(i, carry):
-        for p in range(4):
-
-            @pl.when(o_target(head_at(i), p) != me)
-            def _():
-                for copy in o_copies(i, p):
-                    copy.wait_send()
-
-        return carry
-
-    lax.fori_loop(0, x_count, sums_left, 0)
+    for n in range(len(steps)):
+        rs_copy(n).start()
+
+    left(o_in, o_send)
+    left(stat_in, stat_send)
     share_heads.wait_send()
 
     results = []
@@ -528,21 +523,17 @@
             own = hid[:, pl.ds(pl.multiple_of(start, strip), strip)]
             result = result + dot(spread(16, chip * 4, q), own)
         results.append(result)
-    for k in range(strips):
-        part = pl.ds(k * strip, strip)
-
-        for n in reversed(range(len(steps))):
-            source = chip_at(n)
-            arrived(rs_in.at[source, :, part], rs_recv.at[k, source])
-            results[k] = results[k] + rs_in[source, :, part].astype(F32)
+    arrived(rs_in.at[pl.ds(0, chips - 1)], rs_recv)
     result = jnp.concatenate(results, axis=1)
+    for n in range(len(steps)):
+        result = result + rs_in[chip_at(n)].astype(F32)
 
     def fin_copy(c):
         return pltpu.make_async_remote_copy(
             src_ref=fin_out.at[c],
             dst_ref=fin_in.at[core],
-            send_sem=fin_send.at[c],
-            recv_sem=fin_recv.at[core],
+            send_sem=fin_send,
+            recv_sem=fin_recv,
             device_id={"section": after, "kv": chip * 2 + c},
             device_id_type=MESH,
         )
@@ -554,11 +545,8 @@
         ).astype(BF16)
         fin_copy(c).start()
 
-    for k in range(strips):
-        for n in range(len(steps)):
-            rs_copy(n, k).wait_send()
-    for c in range(2):
-        arrived(fin_in.at[c], fin_recv.at[c])
+    arrived(rs_in.at[pl.ds(0, chips - 1)], rs_send)
+    arrived(fin_in, fin_recv)
     final = []
     for c in range(2):
         rows_in = fin_in[c].astype(F32)
@@ -566,8 +554,7 @@
             for h in range(2):
                 final.append(rows_in[h * 8 + q * 2 : h * 8 + q * 2 + 2])
     out[0] = jnp.concatenate(final, axis=1)
-    for c in range(2):
-        fin_copy(c).wait_send()
+    arrived(fin_out, fin_send)
 
 
 def local(sections, kv_count, *args):
@@ -577,7 +564,6 @@
     x_count, chips = kv_count // 8, kv_count // 2
     pair, wide = 2 * rows, 8 * rows
     lanes = width // 8
-    strips = 2
     pieces = 4
     dma = pltpu.SemaphoreType.DMA
     out = pl.pallas_call(
@@ -614,20 +600,20 @@
             dma((5,)),
             dma((pieces,)),
             dma((2 * x_count + 1,)),
-            dma((2 * x_count + 1,)),
+            dma((3,)),
             dma((2 * x_count + 1,)),
             dma((2,)),
-            dma((4 * x_count,)),
-            dma((4 * x_count,)),
-            dma((4 * x_count,)),
-            dma((chips,)),
-            dma((4 * x_count,)),
-            dma((chips,)),
+            dma,
+            dma((x_count,)),
+            dma,
             dma((2,)),
-            dma((strips, chips)),
-            dma((strips, chips)),
+            dma,
             dma((2,)),
             dma((2,)),
+            dma,
+            dma,
+            dma,
+            dma,
         ],
         compiler_params=pltpu.CompilerParams(
             collective_id=0, has_side_effects=True, vmem_limit_bytes=60 << 20

time: 53 us -> 51.5 us (0.972)
  Pallas kernels: 51.6 us -> 49.6 us
    pallas_call x1, Pallas kernels: 51.6 us -> 49.6 us  [local(): pl.pallas_call(functools.partial(kernel, sections, kv_count), out_shape=p...]
where the time goes in v3:
time: 51.5 us; the launch traced here: 50.9 us
  Pallas kernels  49.6 us (96%)
  between operations  0.66 us (1%)
  other arithmetic  0.64 us (1%)
    pallas_call x1, Pallas kernels, local(): pl.pallas_call(functools.partial(kernel, sections, kv_count), out_shape=p...  49.6 us

profile of v3, /device:TPU:1, one launch (start us, length us, event | category | flops | bytes accessed | tf_op | source)
XLA Modules:
  0.0 50.9 jit_solution(2248039419881424452)
XLA Ops:
  0.7 49.6 %relay_attention.1 = f32[1,2,8192]{2,1,0:T(2,128)S(1)} custom-call(bf16[1,64,8192]{2,1,0:T(8,128)(2,1)} %hid_h.1, f32[1,8192]{1,0:T(1,128)} %gain_h.1, bf16[1,8192,256]{2,1,0:T(8,128)(2,1)} %wq_h.1, bf16[1,12,256,1024]{3,2,1,0:T(8,128)(2,1)} %key_h.1, bf16[1,12,256,1024]{3,2,1,0:T(8,128)(2,1)} %value_h.1, bf16[1,256,8192]{2,1,0:T(8,128)(2,1)} %wo_h.1, ...), custom_call_target="tpu_custom_call" | custom-call | tf_op jit(solution)/shard_map/relay_attention/pallas_call | solution.py:569
  50.3 0.6 %convert_element_type.3 = bf16[1,2,8192]{2,1,0:T(2,128)(2,1)} convert(f32[1,2,8192]{2,1,0:T(2,128)S(1)} %relay_attention.1) | non-fusion elementwise | flops 16384 | bytes 98304 | tf_op jit(solution)/shard_map/convert_element_type | solution.py:623

commit v4 on v3

--- a/solution.py
+++ b/solution.py
@@ -227,12 +227,10 @@
         )
         return copies
 
-    for copy in own_copies():
-        copy.start()
     pl.semaphore_wait(barrier, kv_count - 1 + 4)
 
     def q_target(n):
-        to_z = lax.rem(z + n, 4)
+        to_z = lax.rem(z + 2 + 3 * n, 4)
         to_x = lax.rem(x + x_count - moved(lax.div(n, 4), to_z), x_count)
         return to_x * 8 + to_z * 2 + side
 
@@ -260,7 +258,10 @@
 
         return carry
 
-    lax.fori_loop(0, 4, send_queries, 0)
+    lax.fori_loop(0, min(8, x_count * 4), send_queries, 0)
+
+    for copy in own_copies():
+        copy.start()
 
     for load in scalar_loads:
         load.wait()
@@ -302,8 +303,6 @@
     ).astype(BF16)
     arrived(blocks.at[1], block_sem.at[1])
     mask_columns(1)
-    if x_count > 1:
-        lax.fori_loop(4, 8, send_queries, 0)
 
     def o_target(slot, p):
         return slot * 8 + (core * 2 + p % 2) * 2 + p // 2
@@ -357,6 +356,9 @@
         slot = head_at(i)
         arrived(values.at[slot, pl.ds(0, slots)], own_sem.at[i * 2 + 1])
         arrived(keys.at[slot, pl.ds(slots, slots)], kv_recv.at[i * 2])
+        arrived(values.at[slot, pl.ds(slots, slots)], kv_recv.at[i * 2 + 1])
+        if not last:
+            await_first(i + 1)
         score(i, 1)
         state = (
             jnp.full((8, wide), PEAK_FLOOR, F32),
@@ -364,9 +366,7 @@
             jnp.zeros((HD, wide), F32),
         )
         state = weigh(i, 0, state, pl.ds(0, wide))
-        arrived(values.at[slot, pl.ds(slots, slots)], kv_recv.at[i * 2 + 1])
         if not last:
-            await_first(i + 1)
             score(i + 1, 0)
         cuts = 2 if last else 1
         for cut in range(cuts):
@@ -419,11 +419,9 @@
         def _():
             arrived(ref, sem)
 
-    left(o_in, q_send)
-    send_blocks.wait_send()
-    arrived(keys.at[:, pl.ds(slots, slots)], kv_send.at[0])
-    arrived(values.at[:, pl.ds(slots, slots)], kv_send.at[1])
-    arrived(wo.at[core], kv_send.at[2])
+
+    arrived(wo.at[core], own_sem.at[2 * x_count])
+    arrived(wo.at[other], kv_recv.at[2 * x_count])
 
     def join(state, columns):
         peak, total, summed = state
@@ -485,31 +483,35 @@
     def chip_at(n):
         return lax.rem(x + steps[n][0], x_count) * 4 + lax.rem(z + steps[n][1], 4)
 
-    def rs_copy(n):
+    def rs_copy(n, k):
         to = chip_at(n)
+        part = pl.ds(k * strip, strip)
         return pltpu.make_async_remote_copy(
-            src_ref=rs_out.at[to],
-            dst_ref=rs_in.at[chip],
+            src_ref=rs_out.at[to, :, part],
+            dst_ref=rs_in.at[chip, :, part],
             send_sem=rs_send,
-            recv_sem=rs_recv,
+            recv_sem=rs_recv.at[k],
             device_id={"kv": to * 2 + core},
             device_id_type=MESH,
         )
 
-    arrived(wo.at[core], own_sem.at[2 * x_count])
     parts = spread_heads(core)
     for k in range(strips):
         acc[:, pl.ds(k * strip, strip)] = project(core, parts, k)
-    arrived(wo.at[other], kv_recv.at[2 * x_count])
     arrived(attended.at[other], att_sem.at[1])
     parts = spread_heads(other)
     for k in range(strips):
         part = pl.ds(k * strip, strip)
         term = acc[:, part] + project(other, parts, k)
         rs_out[:, :, part] = term.astype(BF16).reshape(chips, 16, strip)
-    for n in range(len(steps)):
-        rs_copy(n).start()
-
+        for n in range(len(steps)):
+            rs_copy(n, k).start()
+
+    left(o_in, q_send)
+    send_blocks.wait_send()
+    arrived(keys.at[:, pl.ds(slots, slots)], kv_send.at[0])
+    arrived(values.at[:, pl.ds(slots, slots)], kv_send.at[1])
+    arrived(wo.at[core], kv_send.at[2])
     left(o_in, o_send)
     left(stat_in, stat_send)
     share_heads.wait_send()
@@ -523,7 +525,8 @@
             own = hid[:, pl.ds(pl.multiple_of(start, strip), strip)]
             result = result + dot(spread(16, chip * 4, q), own)
         results.append(result)
-    arrived(rs_in.at[pl.ds(0, chips - 1)], rs_recv)
+    for k in range(strips):
+        arrived(rs_in.at[pl.ds(0, chips - 1), :, pl.ds(k * strip, strip)], rs_recv.at[k])
     result = jnp.concatenate(results, axis=1)
     for n in range(len(steps)):
         result = result + rs_in[chip_at(n)].astype(F32)
@@ -611,7 +614,7 @@
             dma((2,)),
             dma((2,)),
             dma,
-            dma,
+            dma((max(1, lanes // 512),)),
             dma,
             dma,
         ],

time: 51.5 us -> 48.7 us (0.946)
  Pallas kernels: 49.6 us -> 47.3 us
    pallas_call x1, Pallas kernels: 49.6 us -> 47.3 us  [local(): pl.pallas_call(functools.partial(kernel, sections, kv_count), out_shape=p...]
where the time goes in v4:
time: 48.7 us; the launch traced here: 48.6 us
  Pallas kernels  47.3 us (97%)
  between operations  0.66 us (1%)
  other arithmetic  0.64 us (1%)
    pallas_call x1, Pallas kernels, local(): pl.pallas_call(functools.partial(kernel, sections, kv_count), out_shape=p...  47.3 us

profile of v4, /device:TPU:1, one launch (start us, length us, event | category | flops | bytes accessed | tf_op | source)
XLA Modules:
  0.0 48.6 jit_solution(11183669665753031807)
XLA Ops:
  0.7 47.3 %relay_attention.1 = f32[1,2,8192]{2,1,0:T(2,128)S(1)} custom-call(bf16[1,64,8192]{2,1,0:T(8,128)(2,1)} %hid_h.1, f32[1,8192]{1,0:T(1,128)} %gain_h.1, bf16[1,8192,256]{2,1,0:T(8,128)(2,1)} %wq_h.1, bf16[1,12,256,1024]{3,2,1,0:T(8,128)(2,1)} %key_h.1, bf16[1,12,256,1024]{3,2,1,0:T(8,128)(2,1)} %value_h.1, bf16[1,256,8192]{2,1,0:T(8,128)(2,1)} %wo_h.1, ...), custom_call_target="tpu_custom_call" | custom-call | tf_op jit(solution)/shard_map/relay_attention/pallas_call | solution.py:572
  48.0 0.6 %convert_element_type.3 = bf16[1,2,8192]{2,1,0:T(2,128)(2,1)} convert(f32[1,2,8192]{2,1,0:T(2,128)S(1)} %relay_attention.1) | non-fusion elementwise | flops 16384 | bytes 98304 | tf_op jit(solution)/shard_map/convert_element_type | solution.py:626
